TPU v7x, 32 devices: a whole 2x2x4 slice. The times are simulated.
32 devices in a mesh: parts: 2 (over y), blk: 4 (over z), dp: 2 (over x), sub: 2 (over core).
Axes of the slice: x: 2, y: 2, z: 4, core: 2. Of those that a mesh axis runs over, the one named last changes fastest.
Arguments:
- in_factors: bfloat16 [2, 4, 512, 1024], P(None, ('parts', 'dp'), 'blk'), parts along dimension 1, may hold values from -6 to 6
- out_factors: bfloat16 [2, 4, 512, 1024], P(None, ('parts', 'dp'), 'blk'), parts along dimension 1, may hold values from -0.75 to 0.75
- lengths: int32 [4, 32], P(('parts', 'dp')), parts along dimension 0, may hold values from 1 to 64, 512 in all within a row
- signs: int32 [2, 1024, 1024], P(None, 'blk'), may hold values 0 or 1
- projection: bfloat16 [2, 1024, 16, 4096], P(None, 'blk', None, 'sub'), may hold values from -0.046875 to 0.046875
Outputs:
- features: float32 [4, 32, 2, 4096], P(('parts', 'dp'), 'blk', None, 'sub'), parts along dimension 0
There are 2 independent parts, one for each index of `parts`. A program takes and returns all parts, laid end to end along the dimension named above; an argument that names none is the same for every part. Nothing has to cross between parts.
Inputs may be any that keep to these rules, and one draw needn't show every extreme that they name: In each row the 32 lengths sum to 512; the documents follow one another over the tokens of their dp index in order.
All inputs are finite; a program needn't handle non-finite values. No bound on the sum of `signs` on one device may be relied on, other than what follows from the above.
Results may differ from a plain program's by a relative error of at most 0.0029.
Values may be sent and summed in bfloat16 or wider, within the bound.
A program may use at most 128 MiB of HBM per device.

v0:
```python
import math

import jax
import jax.numpy as jnp
from jax import lax
from jax.sharding import PartitionSpec as P


def swapped(block, axis, bit):
    count = lax.axis_size(axis)
    route = []
    for low in range(count):
        high = low | 1 << bit
        if high != low and high < count:
            route += [(low, high), (high, low)]
    return lax.ppermute(block, axis, route)


def parity_sign(values):
    total = jnp.zeros_like(values)
    for bit_level in range(16):
        total = total + jnp.bitwise_and(jnp.right_shift(values, bit_level), 1)
    return (1 - 2 * (total % 2)).astype(jnp.float32)


def parity_table(row_ids, col_ids):
    return parity_sign(jnp.bitwise_and(row_ids[:, None], col_ids[None, :]))


def build_weighted(owners, example_ids, input_cols):
    one_hot = (owners[:, None] == example_ids[None, :]).astype(jnp.bfloat16)
    product = one_hot[None, :, :, None] * input_cols[:, 0, :, None, :]
    return product.reshape(product.shape[0], product.shape[1], product.shape[2] * product.shape[3])


def make_accumulate(weighted, portion):
    return jnp.einsum("ltx,ltc->lxc", weighted, portion[:, 0], preferred_element_type=jnp.float32)


def shards(in_factors, out_factors, lengths, signs, projection):
    blocks = lax.axis_size("blk")
    halves = lax.axis_size("sub")
    my_block = lax.axis_index("blk")
    my_half = lax.axis_index("sub")
    layers = in_factors.shape[0]
    tok_local = in_factors.shape[2]
    in_width = in_factors.shape[3]
    out_width = out_factors.shape[3]
    rows_block = in_width // blocks
    documents = lengths.shape[1]
    kept_cols = projection.shape[2]
    tok_shard = tok_local * blocks
    norm_scale = 1.0 / math.sqrt(in_width * out_width)
    input_cols = lax.all_to_all(in_factors, "blk", split_axis=3, concat_axis=2, tiled=True)
    doc_ends = jnp.cumsum(lengths[0])
    positions = jnp.arange(tok_shard, dtype=jnp.int32)
    owners = jnp.sum((positions[:, None] >= doc_ends[None, :]).astype(jnp.int32), axis=1)
    width_part = out_width // halves
    col_base = my_half * width_part
    example_ids = jnp.arange(documents, dtype=jnp.int32)
    right_part = lax.dynamic_slice_in_dim(out_factors, col_base, width_part, 3)
    weighted = build_weighted(owners, example_ids, input_cols)
    gradients = make_accumulate(weighted, lax.all_gather(right_part, "blk", axis=2, tiled=True))
    gradients = gradients.reshape(layers, documents, rows_block, width_part)
    col_ids = col_base + jnp.arange(width_part, dtype=jnp.int32)
    sign_slice = lax.dynamic_slice_in_dim(signs, col_base, width_part, 2)
    signed = (2 * sign_slice - 1).astype(jnp.float32)
    col_mix = parity_table(col_ids, jnp.arange(kept_cols, dtype=jnp.int32))
    mixing = signed[:, :, :, None] * col_mix[None, None, :, :]
    folded = jnp.einsum("leic,lick->leik", gradients, mixing, precision=lax.Precision.HIGHEST)
    local_rows = jnp.arange(rows_block, dtype=jnp.int32)
    row_mix = parity_table(local_rows, local_rows)
    within = jnp.einsum("ji,leik->lejk", row_mix, folded, precision=lax.Precision.HIGHEST)
    within = within.reshape(layers, documents, rows_block * kept_cols)
    within = lax.psum_scatter(within, "sub", scatter_dimension=1, tiled=True)
    blended = within
    for bit_level in range(blocks.bit_length() - 1):
        partner = swapped(blended, "blk", bit_level)
        high_bit = jnp.bitwise_and(jnp.right_shift(my_block, bit_level), 1)
        blended = partner + (1 - 2 * high_bit).astype(jnp.float32) * blended
    kept_half = (blended * norm_scale).astype(jnp.bfloat16)
    gathered = lax.all_gather(kept_half, "sub", axis=1, tiled=True)
    weights = projection.reshape(layers, rows_block * kept_cols, projection.shape[3])
    features = lax.psum_scatter(
        jnp.einsum("lek,lkp->elp", gathered, weights, preferred_element_type=jnp.float32),
        "blk",
        scatter_dimension=0,
        tiled=True,
    )
    return features[None]


def solution(mesh):
    return jax.shard_map(
        shards,
        mesh=mesh,
        in_specs=(
            P(None, ("parts", "dp"), "blk", None),
            P(None, ("parts", "dp"), "blk", None),
            P(("parts", "dp"), None),
            P(None, "blk", None),
            P(None, "blk", None, "sub"),
        ),
        out_specs=P(("parts", "dp"), "blk", None, "sub"),
        check_vma=False,
    )
```

profile of v0, /device:TPU:0, one launch (start us, length us, event | category | flops | bytes accessed | tf_op | source)
XLA Modules:
  0.0 233.8 jit_solution(1665426962694286551)
XLA Ops:
  6.5 1.0 copy-done
  7.6 0.7 constant_dynamic-slice_fusion
  8.3 2.0 copy.37
  10.3 6.3 %all-to-all-start = ((bf16[2,1,128,1024]{2,0,1,3:T(2,128)(2,1)}), bf16[2,1,128,1024]{2,0,1,3:T(2,128)(2,1)S(1)}, u32[]{:S(2)}, u32[]{:S(2)}) async-start(bf16[2,1,128,1024]{2,0,1,3:T(2,128)(2,1)} %copy.37), calls=%async_computation | async-start | bytes 1048576 | tf_op jit(solution)/shard_map/all_to_all | solution.py:54
  16.6 0.7 copy.36
  17.4 0.1 reduce
  17.5 0.1 convert_reduce_fusion
  17.6 1.4 add_convert_fusion
  19.1 0.1 fusion.41
  19.1 23.7 %all-to-all-done = bf16[2,1,128,1024]{2,0,1,3:T(2,128)(2,1)S(1)} async-done(((bf16[2,1,128,1024]{2,0,1,3:T(2,128)(2,1)}), bf16[2,1,128,1024]{2,0,1,3:T(2,128)(2,1)S(1)}, u32[]{:S(2)}, u32[]{:S(2)}) %all-to-all-start) | async-done | bytes 524320 | tf_op jit(solution)/shard_map/all_to_all | solution.py:54
  42.9 0.1 copy.38
  42.9 0.2 copy.39
  43.2 0.2 copy.40
  43.4 0.6 mul.85
  44.0 7.6 %bitcast_multiply_fusion = bf16[2,512,8192]{1,2,0:T(8,128)(2,1)} fusion(bf16[2,512,256]{1,2,0:T(8,128)(2,1)S(1)} %copy.40, bf16[512,8192]{0,1:T(8,128)(2,1)S(1)} %bitcast.34), kind=kLoop, calls=%fused_computation.2 | loop fusion | flops 8388608 | bytes 25690112 | tf_op jit(solution)/shard_map/mul | solution.py:32
  51.6 18.9 %fusion.10 = f32[2,8192,512]{2,1,0:T(8,128)} fusion(bf16[2,512,8192]{1,2,0:T(8,128)(2,1)} %bitcast_multiply_fusion, bf16[2,1,512,512]{3,2,0,1:T(8,128)(2,1)} %all-gather.2.cloned.1.call-done), kind=kOutput, calls=%fused_computation.9 | convolution fusion | flops 8589934592 | bytes 51380224 | tf_op jit(solution)/shard_map/ltx,ltc->lxc/dot_general | solution.py:37
  70.5 54.3 %fusion.5 = f32[2,32,256,16]{1,3,2,0:T(8,128)} fusion(f32[2,32,256,512]{3,2,1,0:T(8,128)} %bitcast.32, f32[512,16]{0,1:T(8,128)S(1)} %fusion.41, f32[2,256,512]{2,1,0:T(8,128)S(1)} %add_convert_fusion), kind=kOutput, calls=%fused_computation.7 | convolution fusion | flops 1614807040 | bytes 35684352 | tf_op jit(solution)/shard_map/leic,lick->leik/dot_general | solution.py:70
  124.8 4.0 %copy.43 = f32[2,32,256,16]{2,3,1,0:T(8,128)S(1)} copy(f32[2,32,256,16]{1,3,2,0:T(8,128)} %fusion.5) | data formatting | bytes 2097152 | tf_op jit(solution)/shard_map/leic,lick->leik/transpose | solution.py:70
  128.8 1.5 convolution_bitcast_fusion.1
  130.3 3.9 %copy.44 = f32[2,32,256,16]{1,3,2,0:T(8,128)} copy(f32[2,32,256,16]{2,3,1,0:T(8,128)S(1)} %convolution_bitcast_fusion.1) | data formatting | bytes 2097152 | tf_op jit(solution)/shard_map/ji,leik->lejk/transpose | solution.py:73
  134.2 3.6 %copy.45 = f32[2,32,4096]{2,1,0:T(8,128)} copy(f32[2,32,4096]{1,2,0:T(8,128)} %bitcast.35) | data formatting | bytes 2097152 | tf_op jit(solution)/shard_map/reshape | solution.py:74
  137.9 7.2 %reduce-scatter.3.cloned.1.call-done = f32[2,16,4096]{2,1,0:T(8,128)} async-done(((f32[2,32,4096]{2,1,0:T(8,128)}), f32[2,16,4096]{2,1,0:T(8,128)}) %reduce-scatter.3.cloned.1.call-update) | async-done | bytes 524304 | tf_op jit(solution)/shard_map/reduce_scatter | solution.py:75
  145.0 1.7 collective-permute-start
  146.8 12.6 %collective-permute-done = f32[2,16,4096]{2,1,0:T(8,128)S(1)} collective-permute-done((f32[2,16,4096]{2,1,0:T(8,128)}, f32[2,16,4096]{2,1,0:T(8,128)S(1)}, u32[]{:S(2)}, u32[]{:S(2)}) %collective-permute-start) | collective-permute-done | bytes 524320 | tf_op jit(solution)/shard_map/ppermute | solution.py:16
  159.4 1.1 multiply_add_fusion
  160.5 2.7 %collective-permute-start.1 = (f32[2,16,4096]{2,1,0:T(8,128)S(1)}, f32[2,16,4096]{2,1,0:T(8,128)S(1)}, u32[]{:S(2)}, u32[]{:S(2)}) collective-permute-start(f32[2,16,4096]{2,1,0:T(8,128)S(1)} %multiply_add_fusion), channel_id=1, source_target_pairs={{0,8},{8,0},{4,12},{12,4},{1,9},{9,1},{5,13},{13,5},{2,10},{10,2},... | collective-permute-start | bytes 1572872 | tf_op jit(solution)/shard_map/ppermute | solution.py:16
  163.2 22.8 %collective-permute-done.1 = f32[2,16,4096]{2,1,0:T(8,128)S(1)} collective-permute-done((f32[2,16,4096]{2,1,0:T(8,128)S(1)}, f32[2,16,4096]{2,1,0:T(8,128)S(1)}, u32[]{:S(2)}, u32[]{:S(2)}) %collective-permute-start.1) | collective-permute-done | bytes 524320 | tf_op jit(solution)/shard_map/ppermute | solution.py:16
  186.0 0.1 multiply_convert_fusion
  186.1 2.2 all_gather.7
  188.3 14.4 %convolution_bitcast_fusion = f32[32,2,2048]{2,0,1:T(8,128)} fusion(bf16[2,32,4096]{2,1,0:T(8,128)(2,1)S(1)} %all_gather.7, bf16[2,4096,2048]{2,1,0:T(8,128)(2,1)} %bitcast.33), kind=kOutput, calls=%fused_computation.6 | convolution fusion | flops 1073741824 | bytes 34603008 | tf_op jit(solution)/shard_map/lek,lkp->elp/dot_general | solution.py:85
  202.7 22.9 %reduce-scatter.5.cloned.1.call-done = f32[8,2,2048]{2,0,1:T(8,128)} async-done(((f32[32,2,2048]{2,0,1:T(8,128)}), f32[8,2,2048]{2,0,1:T(8,128)}) %reduce-scatter.5.cloned.1.call-update) | async-done | bytes 131088 | tf_op jit(solution)/shard_map/reduce_scatter | solution.py:84
  225.6 1.7 copy.46
  (13 shorter events, 0.2 us)
Async XLA Ops:
  6.5 1.0 copy-start
  6.5 45.1 %all-gather.2.cloned.1.call-start = ((), (), s32[]{:S(2)}) async-start(), calls=%async_computation.3 | async-start | bytes 1310720 | tf_op jit(solution)/shard_map/all_gather | solution.py:63
  10.3 32.5 %all-to-all-start = ((bf16[2,1,128,1024]{2,0,1,3:T(2,128)(2,1)}), bf16[2,1,128,1024]{2,0,1,3:T(2,128)(2,1)S(1)}, u32[]{:S(2)}, u32[]{:S(2)}) async-start(bf16[2,1,128,1024]{2,0,1,3:T(2,128)(2,1)} %copy.37), calls=%async_computation | async-start | bytes 1048576 | tf_op jit(solution)/shard_map/all_to_all | solution.py:54
  16.6 128.4 %reduce-scatter.3.cloned.1.call-start = ((), (), s32[]{:S(2)}) async-start(), calls=%async_computation.4 | async-start | bytes 1572864 | tf_op jit(solution)/shard_map/reduce_scatter | solution.py:75
  137.8 87.8 %reduce-scatter.5.cloned.1.call-start = ((), (), s32[]{:S(2)}) async-start(), calls=%async_computation.5 | async-start | bytes 655360 | tf_op jit(solution)/shard_map/reduce_scatter | solution.py:84
  145.0 14.3 %collective-permute-start = (f32[2,16,4096]{2,1,0:T(8,128)}, f32[2,16,4096]{2,1,0:T(8,128)S(1)}, u32[]{:S(2)}, u32[]{:S(2)}) collective-permute-start(f32[2,16,4096]{2,1,0:T(8,128)} %reduce-scatter.3.cloned.1.call-done), channel_id=1, source_target_pairs={{0,4},{4,0},{8,12},{12,8},{1,5},{5,1},{9,13},{13,9},{2,6},{6,2},{1... | collective-permute-start | bytes 1572872 | tf_op jit(solution)/shard_map/ppermute | solution.py:16
  160.5 25.6 %collective-permute-start.1 = (f32[2,16,4096]{2,1,0:T(8,128)S(1)}, f32[2,16,4096]{2,1,0:T(8,128)S(1)}, u32[]{:S(2)}, u32[]{:S(2)}) collective-permute-start(f32[2,16,4096]{2,1,0:T(8,128)S(1)} %multiply_add_fusion), channel_id=1, source_target_pairs={{0,8},{8,0},{4,12},{12,4},{1,9},{9,1},{5,13},{13,5},{2,10},{10,2},... | collective-permute-start | bytes 1572872 | tf_op jit(solution)/shard_map/ppermute | solution.py:16
  188.3 39.0 %copy-start.1 = (bf16[2,1,128,1024]{3,2,1,0:T(8,128)(2,1)S(1)}, bf16[2,1,128,1024]{3,2,1,0:T(8,128)(2,1)}, u32[]{:S(2)}) copy-start(bf16[2,1,128,1024]{3,2,1,0:T(8,128)(2,1)} %param.6) | copy-start | bytes 1572868
Sparse Core Ops, SparseCore 0:
  8.9 39.3 all-gather.1
  138.0 7.0 reduce-scatter.2
  202.8 22.7 reduce-scatter.4
where the time goes:
time: 234 us
  waiting for transfers between devices  89.3 us (38%)
  matrix products  89.1 us (38%)
  local copies, waits for them, and re-layouts  18.8 us (8%)
  between operations  13.2 us (6%)
  starting transfers between devices  10.8 us (5%)
  other arithmetic  10.5 us (4%)
    dot_general x1, matrix products, shards(): jnp.einsum('leic,lick->leik', gradients, mixing, precision=lax.Precision....  54.3 us
    ppermute x2, waiting for transfers between devices, swapped(): return lax.ppermute(block, axis, route)  35.4 us
    all_to_all x1, waiting for transfers between devices, shards(): lax.all_to_all(in_factors, 'blk', split_axis=3, concat_axis=2, tiled=True)  23.7 us
    reduce_scatter x1, waiting for transfers between devices, shards(): lax.psum_scatter(jnp.einsum('lek,lkp->elp', gathered, weights, preferred_...  22.9 us
    dot_general x1, matrix products, make_accumulate(): jnp.einsum('ltx,ltc->lxc', weighted, portion[:, 0], preferred_element_typ...  18.9 us
    dot_general x1, matrix products, shards(): jnp.einsum('lek,lkp->elp', gathered, weights, preferred_element_type=jnp....  14.4 us
    mul x1, other arithmetic, build_weighted(): product = one_hot[None, :, :, None] * input_cols[:, 0, :, None, :]  7.57 us
    reduce_scatter x1, waiting for transfers between devices, shards(): within = lax.psum_scatter(within, 'sub', scatter_dimension=1, tiled=True)  7.15 us
  transfers between devices with their start and end apart: 6, of which 5 were waited for; matrix products, arithmetic and copies ran while one was open for 6% of the time, Pallas kernels for 0%

commit v1 on v0

--- a/solution.py
+++ b/solution.py
@@ -1,9 +1,14 @@
+import functools
 import math
 
 import jax
 import jax.numpy as jnp
 from jax import lax
+from jax.experimental import pallas as pl
+from jax.experimental.pallas import tpu as pltpu
 from jax.sharding import PartitionSpec as P
+
+MESH = pl.DeviceIdType.MESH
 
 
 def swapped(block, axis, bit):
@@ -90,9 +95,330 @@
     return features[None]
 
 
+def parity(values):
+    for shift in (8, 4, 2, 1):
+        values = jnp.bitwise_xor(values, jnp.right_shift(values, shift))
+    return jnp.bitwise_and(values, 1)
+
+
+def pm_one(values):
+    return (1 - 2 * parity(values)).astype(jnp.float32)
+
+
+def iota(shape, axis):
+    return lax.broadcasted_iota(jnp.int32, shape, axis)
+
+
+def split_terms(value, terms):
+    parts = []
+    for _ in range(terms):
+        part = value.astype(jnp.bfloat16)
+        parts.append(part)
+        value = value - part.astype(jnp.float32)
+    return parts
+
+
+def dot(a, b):
+    return jnp.dot(a, b, preferred_element_type=jnp.float32)
+
+
+def sketch_kernel(dims, len_ref, in_ref, out_ref, signs_ref, proj_ref, feat_ref,
+                  in_all, out_all, sign_buf, sign_t, had, perm, weights, folded, stage_own, stage_rx,
+                  kept, own_feat, feat_tx, feat_rx,
+                  proj_sem, sign_sem, out_recv, out_send, in_recv, in_send,
+                  st_send, st_recv, kept_sem, ft_send, ft_recv):
+    n, halves, layers, tok, width, cols, rows, docs, kc, feats, scale = dims
+    me = lax.axis_index("blk")
+    half = lax.axis_index("sub")
+    other = 1 - half
+    layer = half
+    stages = n.bit_length() - 1
+    pieces = stage_own.shape[1]
+    kper = kc // pieces
+    mine = docs // n
+    gl = perm.shape[0]
+    jl = gl // kc
+    groups = rows // jl
+    kdim = rows * kc
+    hq = feats // 2
+
+    slabs = proj_sem.shape[1]
+    depth = kdim // slabs
+
+    def slab(which, piece):
+        at = pl.ds(piece * depth, depth)
+        return pltpu.make_async_copy(proj_ref.at[which, at], weights.at[which, at], proj_sem.at[which, piece])
+
+    own_out = pltpu.make_async_copy(out_ref.at[layer, 0], out_all.at[me], out_recv.at[me])
+    own_in = pltpu.make_async_copy(in_ref.at[layer, 0, :, pl.ds(pl.multiple_of(me * rows, 128), rows)], in_all.at[me], in_recv.at[me])
+    own_sign = pltpu.make_async_copy(signs_ref.at[layer], sign_buf, sign_sem)
+    own_sign.start()
+    own_out.start()
+    own_in.start()
+
+    barrier = pltpu.get_barrier_semaphore()
+    for step in range(1, n):
+        pl.semaphore_signal(barrier, inc=1, device_id={"blk": lax.rem(me + step, n)}, device_id_type=MESH)
+    pl.semaphore_signal(barrier, inc=1, device_id={"sub": other}, device_id_type=MESH)
+    pl.semaphore_wait(barrier, n)
+
+    def out_copy(src, shard, direction):
+        return pltpu.make_async_remote_copy(
+            src_ref=src, dst_ref=out_all.at[shard], send_sem=out_send.at[direction, shard], recv_sem=out_recv.at[shard],
+            device_id={"blk": me + 1 - 2 * direction}, device_id_type=MESH)
+
+    def in_copy(step):
+        to = lax.rem(me + step, n)
+        return pltpu.make_async_remote_copy(
+            src_ref=in_ref.at[layer, 0, :, pl.ds(pl.multiple_of(to * rows, 128), rows)], dst_ref=in_all.at[me],
+            send_sem=in_send.at[to], recv_sem=in_recv.at[me], device_id={"blk": to}, device_id_type=MESH)
+
+    @pl.when(me < n - 1)
+    def _():
+        out_copy(out_ref.at[layer, 0], me, 0).start()
+
+    @pl.when(me > 0)
+    def _():
+        out_copy(out_ref.at[layer, 0], me, 1).start()
+
+    for step in sorted(range(1, n), key=lambda s: min(s, n - s)):
+        in_copy(step).start()
+
+    for which in range(layers):
+        for piece in range(slabs):
+            slab(which, piece).start()
+
+    had[...] = pm_one(jnp.bitwise_and(iota((rows, rows), 0), iota((rows, rows), 1))).astype(jnp.bfloat16)
+    source, target = iota((gl, gl), 0), iota((gl, gl), 1)
+    perm[...] = jnp.where((source % jl) * kc + source // jl == target, 1.0, 0.0).astype(jnp.bfloat16)
+    spread = jnp.broadcast_to(len_ref[...], (docs, docs)).astype(jnp.float32)
+    row_id, col_id = iota((docs, docs), 0), iota((docs, docs), 1)
+    first = jnp.sum(jnp.where(col_id < row_id, spread, 0.0), axis=1, keepdims=True)
+    last = jnp.sum(jnp.where(col_id <= row_id, spread, 0.0), axis=1, keepdims=True)
+    folded[...] = jnp.zeros_like(folded)
+    own_sign.wait()
+    sign_t[...] = (2 * sign_buf[...] - 1).astype(jnp.float32).T.astype(jnp.bfloat16)
+
+    def visit(turn, carry):
+        step = turn // 2
+        shard = me + step * (1 - 2 * (turn % 2))
+
+        @pl.when(jnp.logical_and(jnp.logical_and(shard >= 0, shard < n), turn != 1))
+        def _():
+            pltpu.make_async_copy(out_all.at[shard], out_all.at[shard], out_recv.at[shard]).wait()
+
+            @pl.when(jnp.logical_and(shard < me, me < n - 1))
+            def _():
+                out_copy(out_all.at[shard], shard, 0).start()
+
+            @pl.when(jnp.logical_and(shard > me, me > 0))
+            def _():
+                out_copy(out_all.at[shard], shard, 1).start()
+
+            pltpu.make_async_copy(in_all.at[shard], in_all.at[shard], in_recv.at[shard]).wait()
+            position = (iota((docs, tok), 1) + shard * tok).astype(jnp.float32)
+            hot = jnp.where(jnp.logical_and(position >= first, position < last), 1.0, 0.0).astype(jnp.bfloat16)
+            hot = jnp.concatenate([hot, hot], axis=1)
+
+            def some(group, carry):
+                right = out_all[shard]
+                left = in_all[shard].astype(jnp.float32)
+                col_ids = iota((1, cols), 1)
+                signed = [
+                    right * pm_one(jnp.bitwise_and(col_ids, group * kper + at)).astype(jnp.bfloat16) for at in range(kper)
+                ]
+                product = dot(jnp.concatenate(signed, axis=0), sign_t[...])
+                for at in range(kper):
+                    terms = split_terms(product[at * tok:(at + 1) * tok] * left, 2)
+                    where = pl.ds(pl.multiple_of((group * kper + at) * docs, docs), docs)
+                    folded[where, :] += dot(hot, jnp.concatenate(terms, axis=0))
+                return carry
+
+            lax.fori_loop(0, pieces, some, 0)
+
+        return carry
+
+    lax.fori_loop(0, 2 * n, visit, 0)
+
+    def stage_copy(stage, piece):
+        bit = 1 << stage
+        partner = me + bit * (1 - 2 * ((me // bit) % 2))
+        return pltpu.make_async_remote_copy(
+            src_ref=stage_own.at[stage, piece], dst_ref=stage_rx.at[stage, piece],
+            send_sem=st_send.at[stage, piece], recv_sem=st_recv.at[stage, piece],
+            device_id={"blk": partner}, device_id_type=MESH)
+
+    span = kper * docs
+    for piece in range(pieces):
+        total = None
+        for term in split_terms(folded[piece * span:(piece + 1) * span, :], 3):
+            value = dot(term, had[...])
+            total = value if total is None else total + value
+        stage_own[0, piece] = total
+        stage_copy(0, piece).start()
+    for stage in range(stages):
+        keep_sign = (1 - 2 * ((me // (1 << stage)) % 2)).astype(jnp.float32)
+        for piece in range(pieces):
+            stage_copy(stage, piece).wait_recv()
+            value = stage_rx[stage, piece] + keep_sign * stage_own[stage, piece]
+            if stage < stages - 1:
+                stage_own[stage + 1, piece] = value
+                stage_copy(stage + 1, piece).start()
+            else:
+                value = (value * scale).astype(jnp.bfloat16).astype(jnp.float32)
+                folded[piece * span:(piece + 1) * span, :] = value
+
+    kl = 128 // jl
+    lane = iota((docs, 128), 1) // jl
+    for group in range(groups):
+        tiles = []
+        for part in range(gl // 128):
+            tile = None
+            for at in range(kl):
+                k = part * kl + at
+                place = group * jl
+                base = place // 128 * 128
+                piece = folded[k * docs:(k + 1) * docs, base:base + 128]
+                shift = (at * jl - (place - base)) % 128
+                if shift:
+                    piece = pltpu.roll(piece, shift, 1)
+                tile = piece if tile is None else jnp.where(lane == at, piece, tile)
+            tiles.append(tile)
+        line = jnp.concatenate(tiles, axis=1).astype(jnp.bfloat16)
+        kept[half, group * docs:(group + 1) * docs, :] = dot(line, perm[...]).astype(jnp.bfloat16)
+    kept_copy = pltpu.make_async_remote_copy(
+        src_ref=kept.at[half], dst_ref=kept.at[half], send_sem=kept_sem.at[0], recv_sem=kept_sem.at[1],
+        device_id={"sub": other}, device_id_type=MESH)
+    kept_copy.start()
+
+    def feat_copy(which, step):
+        to = lax.rem(me + step, n)
+        return pltpu.make_async_remote_copy(
+            src_ref=feat_tx.at[which, to], dst_ref=feat_rx.at[which, me],
+            send_sem=ft_send.at[which, to], recv_sem=ft_recv.at[which, me],
+            device_id={"blk": to}, device_id_type=MESH)
+
+    def feat_arrived(which, step):
+        source = lax.rem(me + step, n)
+        return pltpu.make_async_copy(feat_rx.at[which, source], feat_rx.at[which, source], ft_recv.at[which, source])
+
+    per = depth // gl
+    for turn in range(2):
+        which = half if turn == 0 else other
+        if turn == 1:
+            kept_copy.wait_recv()
+        own_feat[which] = jnp.zeros((docs, feats), jnp.float32)
+
+        def slice_step(piece, carry):
+            slab(which, piece).wait()
+            lhs = jnp.concatenate(
+                [kept[which, pl.ds(pl.multiple_of((piece * per + at) * docs, docs), docs), :] for at in range(per)], axis=1)
+            own_feat[which] += dot(lhs, weights[which, pl.ds(pl.multiple_of(piece * depth, depth), depth), :])
+            return carry
+
+        lax.fori_loop(0, slabs, slice_step, 0)
+        for owner in range(n):
+            low = own_feat[which, owner * mine:(owner + 1) * mine, :hq]
+            high = own_feat[which, owner * mine:(owner + 1) * mine, hq:]
+            feat_tx[which, owner] = jnp.concatenate([low, high], axis=0).astype(jnp.bfloat16)
+        for step in range(1, n):
+            feat_copy(which, step).start()
+
+    for turn in range(2):
+        which = half if turn == 1 else other
+        at = pl.ds(pl.multiple_of(me * mine, mine), mine)
+        low = own_feat[which, at, :hq]
+        high = own_feat[which, at, hq:]
+        for step in range(1, n):
+            feat_arrived(which, step).wait()
+            block = feat_rx[which, lax.rem(me + step, n)].astype(jnp.float32)
+            low = low + block[:mine]
+            high = high + block[mine:]
+        feat_ref[which, :, :hq] = low
+        feat_ref[which, :, hq:] = high
+
+    for shard in range(n):
+        @pl.when(jnp.logical_and(shard <= me, me < n - 1))
+        def _():
+            out_copy(out_all.at[shard], shard, 0).wait_send()
+
+        @pl.when(jnp.logical_and(shard >= me, me > 0))
+        def _():
+            out_copy(out_all.at[shard], shard, 1).wait_send()
+
+    for step in range(1, n):
+        in_copy(step).wait_send()
+        for which in range(2):
+            feat_copy(which, step).wait_send()
+    for stage in range(stages):
+        for piece in range(pieces):
+            stage_copy(stage, piece).wait_send()
+    kept_copy.wait_send()
+
+
+def sketch(in_factors, out_factors, lengths, signs, projection):
+    n = lax.axis_size("blk")
+    halves = lax.axis_size("sub")
+    layers, _, tok, width = in_factors.shape
+    cols = out_factors.shape[3]
+    rows = signs.shape[1]
+    docs = lengths.shape[1]
+    kc = projection.shape[2]
+    feats = projection.shape[3]
+    scale = 1.0 / math.sqrt(width * cols)
+    dims = (n, halves, layers, tok, width, cols, rows, docs, kc, feats, scale)
+    stages = n.bit_length() - 1
+    pieces, slabs, gl = 4, 4, 256
+    kdim = rows * kc
+    bf16, f32, dma = jnp.bfloat16, jnp.float32, pltpu.SemaphoreType.DMA
+    anywhere = pl.BlockSpec(memory_space=pl.ANY)
+    vmem = pl.BlockSpec(memory_space=pltpu.VMEM)
+    features = pl.pallas_call(
+        functools.partial(sketch_kernel, dims),
+        out_shape=jax.ShapeDtypeStruct((layers, docs // n, feats), f32),
+        in_specs=[vmem, anywhere, anywhere, anywhere, anywhere],
+        out_specs=vmem,
+        scratch_shapes=[
+            pltpu.VMEM((n, tok, rows), bf16),
+            pltpu.VMEM((n, tok, cols), bf16),
+            pltpu.VMEM((rows, cols), jnp.int32),
+            pltpu.VMEM((cols, rows), bf16),
+            pltpu.VMEM((rows, rows), bf16),
+            pltpu.VMEM((gl, gl), bf16),
+            pltpu.VMEM((layers, kdim, feats), bf16),
+            pltpu.VMEM((kc * docs, rows), f32),
+            pltpu.VMEM((stages, pieces, kc // pieces * docs, rows), f32),
+            pltpu.VMEM((stages, pieces, kc // pieces * docs, rows), f32),
+            pltpu.VMEM((layers, kdim // gl * docs, gl), bf16),
+            pltpu.VMEM((layers, docs, feats), f32),
+            pltpu.VMEM((layers, n, 2 * docs // n, feats // 2), bf16),
+            pltpu.VMEM((layers, n, 2 * docs // n, feats // 2), bf16),
+            dma((layers, slabs)), dma, dma((n,)), dma((2, n)), dma((n,)), dma((n,)),
+            dma((stages, pieces)), dma((stages, pieces)), dma((2,)), dma((layers, n)), dma((layers, n)),
+        ],
+        compiler_params=pltpu.CompilerParams(collective_id=0, has_side_effects=True, vmem_limit_bytes=56 << 20),
+    )(lengths, in_factors, out_factors, signs, projection.reshape(layers, kdim, feats))
+    return jnp.transpose(features, (1, 0, 2))[None]
+
+
+def pick(in_factors, out_factors, lengths, signs, projection):
+    n = lax.axis_size("blk")
+    layers, _, tok, width = in_factors.shape
+    fits = (
+        n > 1 and n & (n - 1) == 0
+        and layers == 2 and lax.axis_size("sub") == 2
+        and signs.shape[1] % 256 == 0 and tok % 128 == 0
+        and lengths.shape[1] % (8 * n) == 0 and 128 % projection.shape[2] == 0 and projection.shape[2] % 16 == 0
+        and projection.shape[3] % 256 == 0
+        and projection.size * projection.dtype.itemsize <= 36 << 20
+    )
+    run = sketch if fits else shards
+    return run(in_factors, out_factors, lengths, signs, projection)
+
+
 def solution(mesh):
     return jax.shard_map(
-        shards,
+        pick,
         mesh=mesh,
         in_specs=(
             P(None, ("parts", "dp"), "blk", None),

time: 234 us -> 75.4 us (0.32)
  waiting for transfers between devices: 89.3 us -> 0 us
  matrix products: 89.1 us -> 0 us
  Pallas kernels: 0 us -> 73.6 us
  local copies, waits for them, and re-layouts: 18.8 us -> 1.66 us
  between operations: 13.2 us -> 0.01 us
  starting transfers between devices: 10.8 us -> 0 us
  other arithmetic: 10.5 us -> 0 us
    dot_general x4 -> x0, matrix products: 89.1 us -> none  [the longest x1 54.3 us: shards(): jnp.einsum('leic,lick->leik', gradients, mixing, precision=lax.Precision....]
    pallas_call x0 -> x1, Pallas kernels: none -> 73.6 us  [sketch(): pl.pallas_call(functools.partial(sketch_kernel, dims), out_shape=jax.Shap...]
    ppermute x2 -> x0, waiting for transfers between devices: 35.4 us -> none  [swapped(): return lax.ppermute(block, axis, route)]
    reduce_scatter x2 -> x0, waiting for transfers between devices: 30.1 us -> none  [the longest x1 22.9 us: shards(): lax.psum_scatter(jnp.einsum('lek,lkp->elp', gathered, weights, preferred_...]
    all_to_all x1 -> x0, waiting for transfers between devices: 23.7 us -> none  [shards(): lax.all_to_all(in_factors, 'blk', split_axis=3, concat_axis=2, tiled=True)]
    transpose x2 -> x0, local copies, waits for them, and re-layouts: 7.87 us -> none  [the longest x1 4.01 us: shards(): jnp.einsum('leic,lick->leik', gradients, mixing, precision=lax.Precision....]
    mul x1 -> x0, other arithmetic: 7.57 us -> none  [build_weighted(): product = one_hot[None, :, :, None] * input_cols[:, 0, :, None, :]]
    all_to_all x1 -> x0, starting transfers between devices: 6.32 us -> none  [shards(): lax.all_to_all(in_factors, 'blk', split_axis=3, concat_axis=2, tiled=True)]
  transfers between devices with their start and end apart: 6 -> 0, of which waited for: 5 -> 0; matrix products, arithmetic and copies ran while one was open for 6% -> 0% of each run, Pallas kernels for 0% -> 0%
where the time goes in v1:
time: 75.4 us; the launch traced here: 75.3 us
  Pallas kernels  73.6 us (98%)
  local copies, waits for them, and re-layouts  1.66 us (2%)
    pallas_call x1, Pallas kernels, sketch(): pl.pallas_call(functools.partial(sketch_kernel, dims), out_shape=jax.Shap...  73.6 us
    broadcast_in_dim x1, local copies, waits for them, and re-layouts, sketch(): return jnp.transpose(features, (1, 0, 2))[None]  1.66 us

profile of v1, /device:TPU:0, one launch (start us, length us, event | category | flops | bytes accessed | tf_op | source)
XLA Modules:
  0.0 75.3 jit_solution(3105682887955414904)
XLA Ops:
  0.0 73.6 %shard_map.55 = f32[2,8,2048]{2,1,0:T(8,128)} custom-call(s32[1,32]{1,0:T(1,128)} %len_ref.1, bf16[2,1,128,1024]{3,2,1,0:T(8,128)(2,1)} %in_ref.1, bf16[2,1,128,1024]{3,2,1,0:T(8,128)(2,1)} %out_ref.1, s32[2,256,1024]{2,1,0:T(8,128)} %signs_ref.1, bf16[2,4096,2048]{2,1,0:T(8,128)(2,1)} %bitcast.4), custom_call_target="tpu_custom_call" | custom-call | tf_op jit(solution)/shard_map/pallas_call | solution.py:376
  73.6 1.7 %copy.6 = f32[1,8,2,2048]{3,2,1,0:T(2,128)} copy(f32[1,8,2,2048]{3,1,2,0:T(8,128)} %bitcast.5) | data formatting | bytes 262144 | tf_op jit(solution)/shard_map/broadcast_in_dim | solution.py:401

commit v2 on v1

--- a/solution.py
+++ b/solution.py
@@ -123,7 +123,7 @@
 
 
 def sketch_kernel(dims, len_ref, in_ref, out_ref, signs_ref, proj_ref, feat_ref,
-                  in_all, out_all, sign_buf, sign_t, had, perm, weights, folded, stage_own, stage_rx,
+                  in_all, out_all, sign_buf, sign_t, had, perm, weights, folded, stage_own, stage_tx, stage_rx, stage_rx16,
                   kept, own_feat, feat_tx, feat_rx,
                   proj_sem, sign_sem, out_recv, out_send, in_recv, in_send,
                   st_send, st_recv, kept_sem, ft_send, ft_recv):
@@ -134,7 +134,8 @@
     layer = half
     stages = n.bit_length() - 1
     pieces = stage_own.shape[1]
-    kper = kc // pieces
+    kper = 4
+    wide = stage_rx.shape[1]
     mine = docs // n
     gl = perm.shape[0]
     jl = gl // kc
@@ -234,7 +235,7 @@
                     folded[where, :] += dot(hot, jnp.concatenate(terms, axis=0))
                 return carry
 
-            lax.fori_loop(0, pieces, some, 0)
+            lax.fori_loop(0, kc // kper, some, 0)
 
         return carry
 
@@ -243,53 +244,44 @@
     def stage_copy(stage, piece):
         bit = 1 << stage
         partner = me + bit * (1 - 2 * ((me // bit) % 2))
+        exact = piece < wide
         return pltpu.make_async_remote_copy(
-            src_ref=stage_own.at[stage, piece], dst_ref=stage_rx.at[stage, piece],
+            src_ref=stage_own.at[stage, piece] if exact else stage_tx.at[stage, piece - wide],
+            dst_ref=stage_rx.at[stage, piece] if exact else stage_rx16.at[stage, piece - wide],
             send_sem=st_send.at[stage, piece], recv_sem=st_recv.at[stage, piece],
             device_id={"blk": partner}, device_id_type=MESH)
 
-    span = kper * docs
+    def stage_send(stage, piece, value):
+        stage_own[stage, piece] = value
+        if piece >= wide:
+            stage_tx[stage, piece - wide] = value.astype(jnp.bfloat16)
+        stage_copy(stage, piece).start()
+
+    def stage_take(stage, piece):
+        stage_copy(stage, piece).wait_recv()
+        if piece < wide:
+            got = stage_rx[stage, piece]
+        else:
+            got = stage_rx16[stage, piece - wide].astype(jnp.float32)
+        keep_sign = (1 - 2 * ((me // (1 << stage)) % 2)).astype(jnp.float32)
+        return got + keep_sign * stage_own[stage, piece]
+
+    ksplit = pieces // (rows // 128)
+    span = kc // ksplit * docs
+
+    def place(piece):
+        return (slice(piece % ksplit * span, (piece % ksplit + 1) * span),
+                slice(piece // ksplit * 128, (piece // ksplit + 1) * 128))
+
     for piece in range(pieces):
         total = None
-        for term in split_terms(folded[piece * span:(piece + 1) * span, :], 3):
-            value = dot(term, had[...])
+        for term in split_terms(folded[place(piece)[0], :], 3):
+            value = dot(term, had[:, place(piece)[1]])
             total = value if total is None else total + value
-        stage_own[0, piece] = total
-        stage_copy(0, piece).start()
-    for stage in range(stages):
-        keep_sign = (1 - 2 * ((me // (1 << stage)) % 2)).astype(jnp.float32)
+        stage_send(0, piece, total)
+    for stage in range(stages - 1):
         for piece in range(pieces):
-            stage_copy(stage, piece).wait_recv()
-            value = stage_rx[stage, piece] + keep_sign * stage_own[stage, piece]
-            if stage < stages - 1:
-                stage_own[stage + 1, piece] = value
-                stage_copy(stage + 1, piece).start()
-            else:
-                value = (value * scale).astype(jnp.bfloat16).astype(jnp.float32)
-                folded[piece * span:(piece + 1) * span, :] = value
-
-    kl = 128 // jl
-    lane = iota((docs, 128), 1) // jl
-    for group in range(groups):
-        tiles = []
-        for part in range(gl // 128):
-            tile = None
-            for at in range(kl):
-                k = part * kl + at
-                place = group * jl
-                base = place // 128 * 128
-                piece = folded[k * docs:(k + 1) * docs, base:base + 128]
-                shift = (at * jl - (place - base)) % 128
-                if shift:
-                    piece = pltpu.roll(piece, shift, 1)
-                tile = piece if tile is None else jnp.where(lane == at, piece, tile)
-            tiles.append(tile)
-        line = jnp.concatenate(tiles, axis=1).astype(jnp.bfloat16)
-        kept[half, group * docs:(group + 1) * docs, :] = dot(line, perm[...]).astype(jnp.bfloat16)
-    kept_copy = pltpu.make_async_remote_copy(
-        src_ref=kept.at[half], dst_ref=kept.at[half], send_sem=kept_sem.at[0], recv_sem=kept_sem.at[1],
-        device_id={"sub": other}, device_id_type=MESH)
-    kept_copy.start()
+            stage_send(stage + 1, piece, stage_take(stage, piece))
 
     def feat_copy(which, step):
         to = lax.rem(me + step, n)
@@ -302,27 +294,60 @@
         source = lax.rem(me + step, n)
         return pltpu.make_async_copy(feat_rx.at[which, source], feat_rx.at[which, source], ft_recv.at[which, source])
 
+    def kept_copy(part):
+        lines = pl.ds(part * (128 // jl) * docs, 128 // jl * docs)
+        return pltpu.make_async_remote_copy(
+            src_ref=kept.at[half, lines], dst_ref=kept.at[half, lines],
+            send_sem=kept_sem.at[0, part], recv_sem=kept_sem.at[1, part],
+            device_id={"sub": other}, device_id_type=MESH)
+
+    kl = 128 // jl
+    lane = iota((docs, 128), 1) // jl
     per = depth // gl
-    for turn in range(2):
-        which = half if turn == 0 else other
-        if turn == 1:
-            kept_copy.wait_recv()
-        own_feat[which] = jnp.zeros((docs, feats), jnp.float32)
-
-        def slice_step(piece, carry):
-            slab(which, piece).wait()
-            lhs = jnp.concatenate(
-                [kept[which, pl.ds(pl.multiple_of((piece * per + at) * docs, docs), docs), :] for at in range(per)], axis=1)
-            own_feat[which] += dot(lhs, weights[which, pl.ds(pl.multiple_of(piece * depth, depth), depth), :])
-            return carry
-
-        lax.fori_loop(0, slabs, slice_step, 0)
-        for owner in range(n):
-            low = own_feat[which, owner * mine:(owner + 1) * mine, :hq]
-            high = own_feat[which, owner * mine:(owner + 1) * mine, hq:]
-            feat_tx[which, owner] = jnp.concatenate([low, high], axis=0).astype(jnp.bfloat16)
-        for step in range(1, n):
-            feat_copy(which, step).start()
+    parts = rows // 128
+    for row_part in range(parts):
+        for piece in range(row_part * ksplit, (row_part + 1) * ksplit):
+            folded[place(piece)] = (stage_take(stages - 1, piece) * scale).astype(jnp.bfloat16).astype(jnp.float32)
+        base = row_part * 128
+        for group in range(row_part * kl, (row_part + 1) * kl):
+            tiles = []
+            for part in range(gl // 128):
+                tile = None
+                for at in range(kl):
+                    k = part * kl + at
+                    piece = folded[k * docs:(k + 1) * docs, base:base + 128]
+                    shift = (at * jl - (group * jl - base)) % 128
+                    if shift:
+                        piece = pltpu.roll(piece, shift, 1)
+                    tile = piece if tile is None else jnp.where(lane == at, piece, tile)
+                tiles.append(tile)
+            line = jnp.concatenate(tiles, axis=1).astype(jnp.bfloat16)
+            kept[half, group * docs:(group + 1) * docs, :] = dot(line, perm[...]).astype(jnp.bfloat16)
+        kept_copy(row_part).start()
+
+        for turn in range(2):
+            which = half if turn == 0 else other
+            if turn == 1:
+                kept_copy(row_part).wait_recv()
+            if row_part == 0:
+                own_feat[which] = jnp.zeros((docs, feats), jnp.float32)
+
+            def slice_step(piece, carry, which=which):
+                slab(which, piece).wait()
+                lhs = jnp.concatenate(
+                    [kept[which, pl.ds(pl.multiple_of((piece * per + at) * docs, docs), docs), :] for at in range(per)],
+                    axis=1)
+                own_feat[which] += dot(lhs, weights[which, pl.ds(pl.multiple_of(piece * depth, depth), depth), :])
+                return carry
+
+            lax.fori_loop(row_part * (slabs // parts), (row_part + 1) * (slabs // parts), slice_step, 0)
+            if row_part == parts - 1:
+                for owner in range(n):
+                    low = own_feat[which, owner * mine:(owner + 1) * mine, :hq]
+                    high = own_feat[which, owner * mine:(owner + 1) * mine, hq:]
+                    feat_tx[which, owner] = jnp.concatenate([low, high], axis=0).astype(jnp.bfloat16)
+                for step in range(1, n):
+                    feat_copy(which, step).start()
 
     for turn in range(2):
         which = half if turn == 1 else other
@@ -353,7 +378,8 @@
     for stage in range(stages):
         for piece in range(pieces):
             stage_copy(stage, piece).wait_send()
-    kept_copy.wait_send()
+    for part in range(parts):
+        kept_copy(part).wait_send()
 
 
 def sketch(in_factors, out_factors, lengths, signs, projection):
@@ -368,7 +394,10 @@
     scale = 1.0 / math.sqrt(width * cols)
     dims = (n, halves, layers, tok, width, cols, rows, docs, kc, feats, scale)
     stages = n.bit_length() - 1
-    pieces, slabs, gl = 4, 4, 256
+    parts = rows // 128
+    pieces, slabs, gl = 2 * parts, 2 * parts, 256
+    wide = pieces // 2
+    span = kc // 2 * docs
     kdim = rows * kc
     bf16, f32, dma = jnp.bfloat16, jnp.float32, pltpu.SemaphoreType.DMA
     anywhere = pl.BlockSpec(memory_space=pl.ANY)
@@ -387,14 +416,16 @@
             pltpu.VMEM((gl, gl), bf16),
             pltpu.VMEM((layers, kdim, feats), bf16),
             pltpu.VMEM((kc * docs, rows), f32),
-            pltpu.VMEM((stages, pieces, kc // pieces * docs, rows), f32),
-            pltpu.VMEM((stages, pieces, kc // pieces * docs, rows), f32),
+            pltpu.VMEM((stages, pieces, span, 128), f32),
+            pltpu.VMEM((stages, pieces - wide, span, 128), bf16),
+            pltpu.VMEM((stages, wide, span, 128), f32),
+            pltpu.VMEM((stages, pieces - wide, span, 128), bf16),
             pltpu.VMEM((layers, kdim // gl * docs, gl), bf16),
             pltpu.VMEM((layers, docs, feats), f32),
             pltpu.VMEM((layers, n, 2 * docs // n, feats // 2), bf16),
             pltpu.VMEM((layers, n, 2 * docs // n, feats // 2), bf16),
             dma((layers, slabs)), dma, dma((n,)), dma((2, n)), dma((n,)), dma((n,)),
-            dma((stages, pieces)), dma((stages, pieces)), dma((2,)), dma((layers, n)), dma((layers, n)),
+            dma((stages, pieces)), dma((stages, pieces)), dma((2, parts)), dma((layers, n)), dma((layers, n)),
         ],
         compiler_params=pltpu.CompilerParams(collective_id=0, has_side_effects=True, vmem_limit_bytes=56 << 20),
     )(lengths, in_factors, out_factors, signs, projection.reshape(layers, kdim, feats))
@@ -408,7 +439,7 @@
         n > 1 and n & (n - 1) == 0
         and layers == 2 and lax.axis_size("sub") == 2
         and signs.shape[1] % 256 == 0 and tok % 128 == 0
-        and lengths.shape[1] % (8 * n) == 0 and 128 % projection.shape[2] == 0 and projection.shape[2] % 16 == 0
+        and lengths.shape[1] % (8 * n) == 0 and projection.shape[2] == 16
         and projection.shape[3] % 256 == 0
         and projection.size * projection.dtype.itemsize <= 36 << 20
     )

time: 75.4 us -> 66.7 us (0.88)
  Pallas kernels: 73.6 us -> 64.8 us
    pallas_call x1, Pallas kernels: 73.6 us -> 64.8 us  [sketch(): pl.pallas_call(functools.partial(sketch_kernel, dims), out_shape=jax.Shap...]
where the time goes in v2:
time: 66.7 us; the launch traced here: 66.5 us
  Pallas kernels  64.8 us (97%)
  local copies, waits for them, and re-layouts  1.66 us (2%)
    pallas_call x1, Pallas kernels, sketch(): pl.pallas_call(functools.partial(sketch_kernel, dims), out_shape=jax.Shap...  64.8 us
    broadcast_in_dim x1, local copies, waits for them, and re-layouts, sketch(): return jnp.transpose(features, (1, 0, 2))[None]  1.66 us

profile of v2, /device:TPU:0, one launch (start us, length us, event | category | flops | bytes accessed | tf_op | source)
XLA Modules:
  0.0 66.5 jit_solution(13748767531418646630)
XLA Ops:
  0.0 64.8 %shard_map.55 = f32[2,8,2048]{2,1,0:T(8,128)} custom-call(s32[1,32]{1,0:T(1,128)} %len_ref.1, bf16[2,1,128,1024]{3,2,1,0:T(8,128)(2,1)} %in_ref.1, bf16[2,1,128,1024]{3,2,1,0:T(8,128)(2,1)} %out_ref.1, s32[2,256,1024]{2,1,0:T(8,128)} %signs_ref.1, bf16[2,4096,2048]{2,1,0:T(8,128)(2,1)} %bitcast.4), custom_call_target="tpu_custom_call" | custom-call | tf_op jit(solution)/shard_map/pallas_call | solution.py:405
  64.9 1.7 %copy.6 = f32[1,8,2,2048]{3,2,1,0:T(2,128)} copy(f32[1,8,2,2048]{3,1,2,0:T(8,128)} %bitcast.5) | data formatting | bytes 262144 | tf_op jit(solution)/shard_map/broadcast_in_dim | solution.py:432

commit v3 on v2

--- a/solution.py
+++ b/solution.py
@@ -141,7 +141,8 @@
     jl = gl // kc
     groups = rows // jl
     kdim = rows * kc
-    hq = feats // 2
+    cuts = feat_tx.shape[1]
+    hq = feats // cuts // 2
 
     slabs = proj_sem.shape[1]
     depth = kdim // slabs
@@ -200,46 +201,62 @@
     own_sign.wait()
     sign_t[...] = (2 * sign_buf[...] - 1).astype(jnp.float32).T.astype(jnp.bfloat16)
 
+    near = jnp.minimum(me, n - 1 - me)
+    longer = 1 - 2 * (me // (n // 2))
+
+    def shard_of(turn):
+        far = jnp.minimum(turn // (2 * near + 1), 1)
+        return me + jnp.maximum((turn + 1) // 2, turn - near) * ((1 - far) * (2 * (turn % 2) - 1) + far * longer)
+
+    def forward(shard):
+        pltpu.make_async_copy(out_all.at[shard], out_all.at[shard], out_recv.at[shard]).wait()
+
+        @pl.when(jnp.logical_and(shard < me, me < n - 1))
+        def _():
+            out_copy(out_all.at[shard], shard, 0).start()
+
+        @pl.when(jnp.logical_and(shard > me, me > 0))
+        def _():
+            out_copy(out_all.at[shard], shard, 1).start()
+
+    def fetch(turn):
+        paired = jnp.logical_and(turn > 0, turn <= 2 * near)
+
+        @pl.when(jnp.logical_not(jnp.logical_and(paired, turn % 2 == 0)))
+        def _():
+            forward(shard_of(turn))
+
+        @pl.when(jnp.logical_and(paired, turn % 2 == 1))
+        def _():
+            forward(shard_of(turn + 1))
+
+        shard = shard_of(turn)
+        pltpu.make_async_copy(in_all.at[shard], in_all.at[shard], in_recv.at[shard]).wait()
+        position = (iota((docs, tok), 1) + shard * tok).astype(jnp.float32)
+        hot = jnp.where(jnp.logical_and(position >= first, position < last), 1.0, 0.0).astype(jnp.bfloat16)
+        return shard, jnp.concatenate([hot, hot], axis=1)
+
+    def add_products(shard, hot, group):
+        right = out_all[shard]
+        left = in_all[shard].astype(jnp.float32)
+        col_ids = iota((1, cols), 1)
+        signed = [right * pm_one(jnp.bitwise_and(col_ids, group * kper + at)).astype(jnp.bfloat16) for at in range(kper)]
+        product = dot(jnp.concatenate(signed, axis=0), sign_t[...])
+        for at in range(kper):
+            terms = split_terms(product[at * tok:(at + 1) * tok] * left, 2)
+            where = pl.ds(pl.multiple_of((group * kper + at) * docs, docs), docs)
+            folded[where, :] += dot(hot, jnp.concatenate(terms, axis=0))
+
     def visit(turn, carry):
-        step = turn // 2
-        shard = me + step * (1 - 2 * (turn % 2))
-
-        @pl.when(jnp.logical_and(jnp.logical_and(shard >= 0, shard < n), turn != 1))
-        def _():
-            pltpu.make_async_copy(out_all.at[shard], out_all.at[shard], out_recv.at[shard]).wait()
-
-            @pl.when(jnp.logical_and(shard < me, me < n - 1))
-            def _():
-                out_copy(out_all.at[shard], shard, 0).start()
-
-            @pl.when(jnp.logical_and(shard > me, me > 0))
-            def _():
-                out_copy(out_all.at[shard], shard, 1).start()
-
-            pltpu.make_async_copy(in_all.at[shard], in_all.at[shard], in_recv.at[shard]).wait()
-            position = (iota((docs, tok), 1) + shard * tok).astype(jnp.float32)
-            hot = jnp.where(jnp.logical_and(position >= first, position < last), 1.0, 0.0).astype(jnp.bfloat16)
-            hot = jnp.concatenate([hot, hot], axis=1)
-
-            def some(group, carry):
-                right = out_all[shard]
-                left = in_all[shard].astype(jnp.float32)
-                col_ids = iota((1, cols), 1)
-                signed = [
-                    right * pm_one(jnp.bitwise_and(col_ids, group * kper + at)).astype(jnp.bfloat16) for at in range(kper)
-                ]
-                product = dot(jnp.concatenate(signed, axis=0), sign_t[...])
-                for at in range(kper):
-                    terms = split_terms(product[at * tok:(at + 1) * tok] * left, 2)
-                    where = pl.ds(pl.multiple_of((group * kper + at) * docs, docs), docs)
-                    folded[where, :] += dot(hot, jnp.concatenate(terms, axis=0))
-                return carry
-
-            lax.fori_loop(0, kc // kper, some, 0)
-
-        return carry
-
-    lax.fori_loop(0, 2 * n, visit, 0)
+        shard, hot = fetch(turn)
+
+        def some(group, carry):
+            add_products(shard, hot, group)
+            return carry
+
+        return lax.fori_loop(0, kc // kper, some, carry)
+
+    lax.fori_loop(0, n - 1, visit, 0)
 
     def stage_copy(stage, piece):
         bit = 1 << stage
@@ -273,26 +290,40 @@
         return (slice(piece % ksplit * span, (piece % ksplit + 1) * span),
                 slice(piece // ksplit * 128, (piece // ksplit + 1) * 128))
 
-    for piece in range(pieces):
+    def local_transform(piece):
         total = None
         for term in split_terms(folded[place(piece)[0], :], 3):
             value = dot(term, had[:, place(piece)[1]])
             total = value if total is None else total + value
         stage_send(0, piece, total)
+
+    shard, hot = fetch(n - 1)
+    for piece in range(ksplit):
+        each = kc // kper // ksplit
+
+        def last_products(group, carry):
+            add_products(shard, hot, group)
+            return carry
+
+        lax.fori_loop(piece * each, (piece + 1) * each, last_products, 0)
+        local_transform(piece)
+    for piece in range(ksplit, pieces):
+        local_transform(piece)
     for stage in range(stages - 1):
         for piece in range(pieces):
             stage_send(stage + 1, piece, stage_take(stage, piece))
 
-    def feat_copy(which, step):
+    def feat_copy(which, cut, step):
         to = lax.rem(me + step, n)
         return pltpu.make_async_remote_copy(
-            src_ref=feat_tx.at[which, to], dst_ref=feat_rx.at[which, me],
-            send_sem=ft_send.at[which, to], recv_sem=ft_recv.at[which, me],
+            src_ref=feat_tx.at[which, cut, to], dst_ref=feat_rx.at[which, cut, me],
+            send_sem=ft_send.at[which, cut, to], recv_sem=ft_recv.at[which, cut, me],
             device_id={"blk": to}, device_id_type=MESH)
 
-    def feat_arrived(which, step):
+    def feat_arrived(which, cut, step):
         source = lax.rem(me + step, n)
-        return pltpu.make_async_copy(feat_rx.at[which, source], feat_rx.at[which, source], ft_recv.at[which, source])
+        block = feat_rx.at[which, cut, source]
+        return pltpu.make_async_copy(block, block, ft_recv.at[which, cut, source])
 
     def kept_copy(part):
         lines = pl.ds(part * (128 // jl) * docs, 128 // jl * docs)
@@ -332,35 +363,44 @@
             if row_part == 0:
                 own_feat[which] = jnp.zeros((docs, feats), jnp.float32)
 
-            def slice_step(piece, carry, which=which):
-                slab(which, piece).wait()
-                lhs = jnp.concatenate(
-                    [kept[which, pl.ds(pl.multiple_of((piece * per + at) * docs, docs), docs), :] for at in range(per)],
-                    axis=1)
-                own_feat[which] += dot(lhs, weights[which, pl.ds(pl.multiple_of(piece * depth, depth), depth), :])
-                return carry
-
-            lax.fori_loop(row_part * (slabs // parts), (row_part + 1) * (slabs // parts), slice_step, 0)
-            if row_part == parts - 1:
-                for owner in range(n):
-                    low = own_feat[which, owner * mine:(owner + 1) * mine, :hq]
-                    high = own_feat[which, owner * mine:(owner + 1) * mine, hq:]
-                    feat_tx[which, owner] = jnp.concatenate([low, high], axis=0).astype(jnp.bfloat16)
-                for step in range(1, n):
-                    feat_copy(which, step).start()
-
-    for turn in range(2):
-        which = half if turn == 1 else other
-        at = pl.ds(pl.multiple_of(me * mine, mine), mine)
-        low = own_feat[which, at, :hq]
-        high = own_feat[which, at, hq:]
-        for step in range(1, n):
-            feat_arrived(which, step).wait()
-            block = feat_rx[which, lax.rem(me + step, n)].astype(jnp.float32)
-            low = low + block[:mine]
-            high = high + block[mine:]
-        feat_ref[which, :, :hq] = low
-        feat_ref[which, :, hq:] = high
+            final = row_part == parts - 1
+            for cut in range(cuts if final else 1):
+                piece_width = feats // cuts if final else feats
+                across = slice(cut * piece_width, (cut + 1) * piece_width)
+
+                def slice_step(piece, carry, which=which, cut=cut, across=across):
+                    if cut == 0:
+                        slab(which, piece).wait()
+                    lhs = jnp.concatenate(
+                        [kept[which, pl.ds(pl.multiple_of((piece * per + at) * docs, docs), docs), :] for at in range(per)],
+                        axis=1)
+                    own_feat[which, :, across] += dot(
+                        lhs, weights[which, pl.ds(pl.multiple_of(piece * depth, depth), depth), across])
+                    return carry
+
+                lax.fori_loop(row_part * (slabs // parts), (row_part + 1) * (slabs // parts), slice_step, 0)
+                if final:
+                    for owner in range(n):
+                        low = own_feat[which, owner * mine:(owner + 1) * mine, cut * piece_width:cut * piece_width + hq]
+                        high = own_feat[which, owner * mine:(owner + 1) * mine, cut * piece_width + hq:(cut + 1) * piece_width]
+                        feat_tx[which, cut, owner] = jnp.concatenate([low, high], axis=0).astype(jnp.bfloat16)
+                    for step in sorted(range(1, n), key=lambda s: -min(s, n - s)):
+                        feat_copy(which, cut, step).start()
+
+    at = pl.ds(pl.multiple_of(me * mine, mine), mine)
+    for which in range(2):
+        for cut in range(cuts):
+            for step in range(1, n):
+                feat_arrived(which, cut, step).wait()
+            begin = cut * 2 * hq
+            low = own_feat[which, at, begin:begin + hq]
+            high = own_feat[which, at, begin + hq:begin + 2 * hq]
+            for step in range(1, n):
+                block = feat_rx[which, cut, lax.rem(me + step, n)].astype(jnp.float32)
+                low = low + block[:mine]
+                high = high + block[mine:]
+            feat_ref[:, which, begin:begin + hq] = low
+            feat_ref[:, which, begin + hq:begin + 2 * hq] = high
 
     for shard in range(n):
         @pl.when(jnp.logical_and(shard <= me, me < n - 1))
@@ -374,7 +414,8 @@
     for step in range(1, n):
         in_copy(step).wait_send()
         for which in range(2):
-            feat_copy(which, step).wait_send()
+            for cut in range(cuts):
+                feat_copy(which, cut, step).wait_send()
     for stage in range(stages):
         for piece in range(pieces):
             stage_copy(stage, piece).wait_send()
@@ -397,6 +438,7 @@
     parts = rows // 128
     pieces, slabs, gl = 2 * parts, 2 * parts, 256
     wide = pieces // 2
+    cuts = 2
     span = kc // 2 * docs
     kdim = rows * kc
     bf16, f32, dma = jnp.bfloat16, jnp.float32, pltpu.SemaphoreType.DMA
@@ -404,7 +446,7 @@
     vmem = pl.BlockSpec(memory_space=pltpu.VMEM)
     features = pl.pallas_call(
         functools.partial(sketch_kernel, dims),
-        out_shape=jax.ShapeDtypeStruct((layers, docs // n, feats), f32),
+        out_shape=jax.ShapeDtypeStruct((docs // n, layers, feats), f32),
         in_specs=[vmem, anywhere, anywhere, anywhere, anywhere],
         out_specs=vmem,
         scratch_shapes=[
@@ -422,14 +464,14 @@
             pltpu.VMEM((stages, pieces - wide, span, 128), bf16),
             pltpu.VMEM((layers, kdim // gl * docs, gl), bf16),
             pltpu.VMEM((layers, docs, feats), f32),
-            pltpu.VMEM((layers, n, 2 * docs // n, feats // 2), bf16),
-            pltpu.VMEM((layers, n, 2 * docs // n, feats // 2), bf16),
+            pltpu.VMEM((layers, cuts, n, 2 * docs // n, feats // cuts // 2), bf16),
+            pltpu.VMEM((layers, cuts, n, 2 * docs // n, feats // cuts // 2), bf16),
             dma((layers, slabs)), dma, dma((n,)), dma((2, n)), dma((n,)), dma((n,)),
-            dma((stages, pieces)), dma((stages, pieces)), dma((2, parts)), dma((layers, n)), dma((layers, n)),
+            dma((stages, pieces)), dma((stages, pieces)), dma((2, parts)), dma((layers, cuts, n)), dma((layers, cuts, n)),
         ],
         compiler_params=pltpu.CompilerParams(collective_id=0, has_side_effects=True, vmem_limit_bytes=56 << 20),
     )(lengths, in_factors, out_factors, signs, projection.reshape(layers, kdim, feats))
-    return jnp.transpose(features, (1, 0, 2))[None]
+    return features[None]
 
 
 def pick(in_factors, out_factors, lengths, signs, projection):
@@ -440,7 +482,7 @@
         and layers == 2 and lax.axis_size("sub") == 2
         and signs.shape[1] % 256 == 0 and tok % 128 == 0
         and lengths.shape[1] % (8 * n) == 0 and projection.shape[2] == 16
-        and projection.shape[3] % 256 == 0
+        and projection.shape[3] % 512 == 0
         and projection.size * projection.dtype.itemsize <= 36 << 20
     )
     run = sketch if fits else shards

time: 66.7 us -> 65.8 us (0.987)
  Pallas kernels: 64.8 us -> 64.1 us
    broadcast_in_dim x1 -> x0, local copies, waits for them, and re-layouts: 1.66 us -> none  [sketch(): return jnp.transpose(features, (1, 0, 2))[None]]
    unnamed x0 -> x1, local copies, waits for them, and re-layouts: none -> 1.57 us
    pallas_call x1, Pallas kernels: 64.8 us -> 64.1 us  [sketch(): pl.pallas_call(functools.partial(sketch_kernel, dims), out_shape=jax.Shap...]
where the time goes in v3:
time: 65.8 us; the launch traced here: 65.7 us
  Pallas kernels  64.1 us (97%)
  local copies, waits for them, and re-layouts  1.57 us (2%)
    pallas_call x1, Pallas kernels, sketch(): pl.pallas_call(functools.partial(sketch_kernel, dims), out_shape=jax.Shap...  64.1 us
    unnamed x1, local copies, waits for them, and re-layouts  1.57 us

profile of v3, /device:TPU:0, one launch (start us, length us, event | category | flops | bytes accessed | tf_op | source)
XLA Modules:
  0.0 65.7 jit_solution(13173100536423229898)
XLA Ops:
  0.0 64.1 %shard_map.55 = f32[8,2,2048]{2,1,0:T(2,128)} custom-call(s32[1,32]{1,0:T(1,128)} %len_ref.1, bf16[2,1,128,1024]{3,2,1,0:T(8,128)(2,1)} %in_ref.1, bf16[2,1,128,1024]{3,2,1,0:T(8,128)(2,1)} %out_ref.1, s32[2,256,1024]{2,1,0:T(8,128)} %signs_ref.1, bf16[2,4096,2048]{2,1,0:T(8,128)(2,1)} %bitcast.2), custom_call_target="tpu_custom_call" | custom-call | tf_op jit(solution)/shard_map/pallas_call | solution.py:447
  64.1 1.6 %copy.7 = f32[1,8,2,2048]{3,2,1,0:T(2,128)} copy(f32[1,8,2,2048]{3,2,1,0:T(2,128)} %bitcast.3) | data formatting | bytes 262144

commit v4 on v3

--- a/solution.py
+++ b/solution.py
@@ -135,7 +135,7 @@
     stages = n.bit_length() - 1
     pieces = stage_own.shape[1]
     kper = 4
-    wide = stage_rx.shape[1]
+    narrow = stage_rx16.shape[1]
     mine = docs // n
     gl = perm.shape[0]
     jl = gl // kc
@@ -185,10 +185,6 @@
 
     for step in sorted(range(1, n), key=lambda s: min(s, n - s)):
         in_copy(step).start()
-
-    for which in range(layers):
-        for piece in range(slabs):
-            slab(which, piece).start()
 
     had[...] = pm_one(jnp.bitwise_and(iota((rows, rows), 0), iota((rows, rows), 1))).astype(jnp.bfloat16)
     source, target = iota((gl, gl), 0), iota((gl, gl), 1)
@@ -250,6 +246,12 @@
     def visit(turn, carry):
         shard, hot = fetch(turn)
 
+        @pl.when(turn == min(1, n - 2))
+        def _():
+            for piece in range(slabs):
+                for which in range(layers):
+                    slab(which, piece).start()
+
         def some(group, carry):
             add_products(shard, hot, group)
             return carry
@@ -261,25 +263,25 @@
     def stage_copy(stage, piece):
         bit = 1 << stage
         partner = me + bit * (1 - 2 * ((me // bit) % 2))
-        exact = piece < wide
+        exact = piece >= narrow
         return pltpu.make_async_remote_copy(
-            src_ref=stage_own.at[stage, piece] if exact else stage_tx.at[stage, piece - wide],
-            dst_ref=stage_rx.at[stage, piece] if exact else stage_rx16.at[stage, piece - wide],
+            src_ref=stage_own.at[stage, piece] if exact else stage_tx.at[stage, piece],
+            dst_ref=stage_rx.at[stage, piece - narrow] if exact else stage_rx16.at[stage, piece],
             send_sem=st_send.at[stage, piece], recv_sem=st_recv.at[stage, piece],
             device_id={"blk": partner}, device_id_type=MESH)
 
     def stage_send(stage, piece, value):
         stage_own[stage, piece] = value
-        if piece >= wide:
-            stage_tx[stage, piece - wide] = value.astype(jnp.bfloat16)
+        if piece < narrow:
+            stage_tx[stage, piece] = value.astype(jnp.bfloat16)
         stage_copy(stage, piece).start()
 
     def stage_take(stage, piece):
         stage_copy(stage, piece).wait_recv()
-        if piece < wide:
-            got = stage_rx[stage, piece]
+        if piece >= narrow:
+            got = stage_rx[stage, piece - narrow]
         else:
-            got = stage_rx16[stage, piece - wide].astype(jnp.float32)
+            got = stage_rx16[stage, piece].astype(jnp.float32)
         keep_sign = (1 - 2 * ((me // (1 << stage)) % 2)).astype(jnp.float32)
         return got + keep_sign * stage_own[stage, piece]
 

time: 65.8 us -> 64.1 us (0.974)
  Pallas kernels: 64.1 us -> 62.3 us
    pallas_call x1, Pallas kernels: 64.1 us -> 62.3 us  [sketch(): pl.pallas_call(functools.partial(sketch_kernel, dims), out_shape=jax.Shap...]
where the time goes in v4:
time: 64.1 us; the launch traced here: 63.9 us
  Pallas kernels  62.3 us (97%)
  local copies, waits for them, and re-layouts  1.57 us (2%)
    pallas_call x1, Pallas kernels, sketch(): pl.pallas_call(functools.partial(sketch_kernel, dims), out_shape=jax.Shap...  62.3 us
    unnamed x1, local copies, waits for them, and re-layouts  1.57 us

profile of v4, /device:TPU:0, one launch (start us, length us, event | category | flops | bytes accessed | tf_op | source)
XLA Modules:
  0.0 63.9 jit_solution(613286273097334575)
XLA Ops:
  0.0 62.3 %shard_map.55 = f32[8,2,2048]{2,1,0:T(2,128)} custom-call(s32[1,32]{1,0:T(1,128)} %len_ref.1, bf16[2,1,128,1024]{3,2,1,0:T(8,128)(2,1)} %in_ref.1, bf16[2,1,128,1024]{3,2,1,0:T(8,128)(2,1)} %out_ref.1, s32[2,256,1024]{2,1,0:T(8,128)} %signs_ref.1, bf16[2,4096,2048]{2,1,0:T(8,128)(2,1)} %bitcast.2), custom_call_target="tpu_custom_call" | custom-call | tf_op jit(solution)/shard_map/pallas_call | solution.py:449
  62.3 1.6 %copy.7 = f32[1,8,2,2048]{3,2,1,0:T(2,128)} copy(f32[1,8,2,2048]{3,2,1,0:T(2,128)} %bitcast.3) | data formatting | bytes 262144
